TPU v7x, 32 devices: a whole 2x2x4 slice. The times are simulated.
32 devices in a mesh: tile: 8 (over z, x), owner: 4 (over y, core).
Axes of the slice: x: 2, y: 2, z: 4, core: 2. Of those that a mesh axis runs over, the one named last changes fastest.
Arguments:
- potential: bfloat16 [2, 8, 1024, 256], P(None, 'tile', 'owner'), may hold values from -6 to 6
- positions: int32 [128, 2], P(('tile', 'owner')), may hold values from 0 to 1792, as said below
- illumination: float32 [2, 256, 256], replicated, may hold values from -5 to 5
- measured: float32 [128, 256, 256], P(('tile', 'owner')), may hold values from 0 to 2
Outputs:
- gradient: float32 [2, 8, 1024, 256], P(None, 'tile', 'owner')
Inputs may be any that keep to these rules, and one draw needn't show every extreme that they name: `positions`: probe p belongs to tile p // 16: its window starts inside that tile and lies inside the object grid, reaching at most into the tiles to the right, below and below-right.
All inputs are finite; a program needn't handle non-finite values.
Results may differ from a plain program's by a relative error of at most 0.0003.
Values may be sent and summed in bfloat16 or wider, within the bound.
A program may use at most 64 MiB of HBM per device.

v0:
```python
import functools
import math

import jax
import jax.numpy as jnp
import numpy as np
from jax import lax
from jax.experimental import pallas as pl
from jax.experimental.pallas import tpu as pltpu
from jax.sharding import PartitionSpec as P

TX = 8

SIGMA = 0.5
LOSS_WEIGHT = 0.125
ALIGN = 16


def passed_along(block, axis, distance):
    devices = range(lax.axis_size(axis))
    route = [(i - distance, i) for i in devices if i - distance in devices]
    return lax.ppermute(block, axis, route)


def block_tables(width):
    counter = np.arange(width)
    signed = (counter + width // 2) % width - width // 2
    angle = 2.0 * np.pi / width * (counter[:, None] * counter[None, :] % width)
    dft = np.exp(-1j * angle) / math.sqrt(width)
    chirp = np.exp(-4j * np.pi * signed.astype(np.float64) ** 2 / (width * width))
    prop = (np.conj(dft) * chirp[None, :]) @ dft

    def right(m):
        return np.block([[m.real, m.imag], [-m.imag, m.real]])

    full = np.stack([right(dft), right(np.conj(dft)), right(prop), right(np.conj(prop))])
    full = full.astype(np.float32)
    high = full.astype(jnp.bfloat16)
    low = (full - high.astype(np.float32)).astype(jnp.bfloat16)
    return high, low


def halves(x):
    high = x.astype(jnp.bfloat16)
    low = (x - high.astype(jnp.float32)).astype(jnp.bfloat16)
    return high, low


def dot3(a, b):
    def dot(x, y):
        return jnp.dot(x, y, preferred_element_type=jnp.float32)

    return dot(a[0], b[0]) + (dot(a[0], b[1]) + dot(a[1], b[0]))


def both_sides(real, imag, high, low, which):
    width = real.shape[0]
    wide = jnp.concatenate([real, imag], axis=1)
    wide = dot3(halves(wide), (high[which], low[which]))
    tall = jnp.concatenate([wide[:, :width], wide[:, width:]], axis=0)
    other = which ^ 1
    tall = dot3((high[other], low[other]), halves(tall))
    return tall[:width], tall[width:]


def turn(window):
    y = (0.5 * SIGMA) * window
    z = y * y
    sine = -1.0 / 39916800.0
    for c in (1.0 / 362880.0, -1.0 / 5040.0, 1.0 / 120.0, -1.0 / 6.0, 1.0):
        sine = sine * z + c
    sine = sine * y
    cosine = 1.0 / 479001600.0
    for c in (-1.0 / 3628800.0, 1.0 / 40320.0, -1.0 / 720.0, 1.0 / 24.0, -0.5, 1.0):
        cosine = cosine * z + c
    return 1.0 - 2.0 * sine * sine, 2.0 * sine * cosine


def probes_kernel(corner_ref, ext_ref, illum_ref, meas_ref, high, low, acc_ref):
    width = illum_ref.shape[1]
    rows, cols = ext_ref.shape[1], ext_ref.shape[2]
    span = width + ALIGN
    acc_ref[...] = jnp.zeros_like(acc_ref)

    def probe(p, carry):
        r = corner_ref[p, 0]
        c = corner_ref[p, 1]
        base = pl.multiple_of(jnp.minimum((r // ALIGN) * ALIGN, rows - span), ALIGN)
        shift = r - base

        def cut(s):
            x = ext_ref[s, pl.ds(base, span), :].astype(jnp.float32)
            x = pltpu.roll(x, span - shift, 0)[:width]
            return pltpu.roll(x, cols - c, 1)[:, :width]

        def paste(s, g):
            x = jnp.concatenate([g, jnp.zeros((width, cols - width), jnp.float32)], axis=1)
            x = pltpu.roll(x, c, 1)
            x = jnp.concatenate([x, jnp.zeros((ALIGN, cols), jnp.float32)], axis=0)
            acc_ref[s, pl.ds(base, span), :] += pltpu.roll(x, shift, 0)

        cos0, sin0 = turn(cut(0))
        first_r = illum_ref[0] * cos0 - illum_ref[1] * sin0
        first_i = illum_ref[0] * sin0 + illum_ref[1] * cos0
        mid_r, mid_i = both_sides(first_r, first_i, high, low, 2)
        cos1, sin1 = turn(cut(1))
        exit_r = mid_r * cos1 - mid_i * sin1
        exit_i = mid_r * sin1 + mid_i * cos1
        far_r, far_i = both_sides(exit_r, exit_i, high, low, 0)
        misfit = far_r * far_r + far_i * far_i - meas_ref[p]
        scale = (4.0 * LOSS_WEIGHT) * misfit
        g_r, g_i = both_sides(scale * far_r, scale * far_i, high, low, 1)
        paste(1, SIGMA * (g_i * exit_r - g_r * exit_i))
        b_r = g_r * cos1 + g_i * sin1
        b_i = g_i * cos1 - g_r * sin1
        g_r, g_i = both_sides(b_r, b_i, high, low, 3)
        paste(0, SIGMA * (g_i * first_r - g_r * first_i))
        return carry

    lax.fori_loop(0, meas_ref.shape[0], probe, 0)


def probe_gradients(corners, extended, illumination, measured, interpret=False):
    high, low = block_tables(illumination.shape[1])
    vmem = pl.BlockSpec(memory_space=pltpu.VMEM)
    probes, width = measured.shape[0], measured.shape[1]
    flops = probes * 4 * 2 * 3 * 2 * (2 * width) ** 2 * width
    return pl.pallas_call(
        probes_kernel,
        out_shape=jax.ShapeDtypeStruct(extended.shape, jnp.float32),
        in_specs=[pl.BlockSpec(memory_space=pltpu.SMEM)] + [vmem] * 5,
        out_specs=vmem,
        compiler_params=pltpu.CompilerParams(vmem_limit_bytes=56 * 2**20),
        cost_estimate=pl.CostEstimate(flops=flops, bytes_accessed=16 * 2**20, transcendentals=0),
        interpret=interpret,
    )(corners, extended, illumination, measured, jnp.asarray(high), jnp.asarray(low))


def body(potential, positions, illumination, measured):
    probe_width = illumination.shape[1]
    rows_part = potential[:, 0]
    tile_rows = rows_part.shape[1] * lax.axis_size("owner")
    tile_cols = rows_part.shape[2]
    below = lax.axis_size("tile") > TX
    right_rim = passed_along(rows_part, "tile", -1)
    extended = lax.all_gather(
        jnp.concatenate([rows_part, right_rim], axis=2), "owner", axis=1, tiled=True
    )
    if below:
        lower_rim = passed_along(extended[:, :probe_width, :], "tile", -TX)
        extended = jnp.concatenate([extended, lower_rim], axis=1)
    tile_id = lax.axis_index("tile")
    first = jnp.stack([tile_id // TX * tile_rows, tile_id % TX * tile_cols])
    corners = positions - first[None, :].astype(jnp.int32)
    accumulated = probe_gradients(corners, extended, illumination, measured)
    wide_grad = accumulated[:, :tile_rows, :]
    if below:
        upper_back = passed_along(accumulated[:, tile_rows:, :], "tile", TX)
        wide_grad = wide_grad.at[:, :probe_width, :].add(upper_back)
    row_shard = lax.psum_scatter(wide_grad, "owner", scatter_dimension=1, tiled=True)
    left_back = passed_along(row_shard[:, :, tile_cols:], "tile", 1)
    result = row_shard[:, :, :tile_cols] + left_back
    return result[:, None]


def solution(mesh):
    in_specs = (
        P(None, "tile", "owner", None),
        P(("tile", "owner"), None),
        P(),
        P(("tile", "owner"), None, None),
    )
    out_specs = P(None, "tile", "owner", None)
    return jax.shard_map(body, mesh=mesh, in_specs=in_specs, out_specs=out_specs, check_vma=False)
```

profile of v0, /device:TPU:0, one launch (start us, length us, event | category | flops | bytes accessed | tf_op | source)
XLA Modules:
  0.0 147.4 jit_solution(6691392777042531515)
XLA Ops:
  6.5 0.0 all-gather.2.cloned.1.call-start
  6.5 1.3 collective-permute-start
  7.8 10.1 %collective-permute-done = bf16[2,256,256]{2,1,0:T(8,128)(2,1)S(1)} collective-permute-done((bf16[2,256,256]{2,1,0:T(8,128)(2,1)}, bf16[2,256,256]{2,1,0:T(8,128)(2,1)S(1)}, u32[]{:S(2)}, u32[]{:S(2)}) %collective-permute-start) | collective-permute-done | bytes 262176 | tf_op jit(solution)/shard_map/ppermute | solution.py:22
  17.9 1.8 %pad_maximum_fusion = bf16[2,256,512]{2,1,0:T(8,128)(2,1)} fusion(bf16[2,256,256]{2,1,0:T(8,128)(2,1)S(1)} %collective-permute-done, bf16[2,256,256]{2,1,0:T(8,128)(2,1)} %bitcast.8), kind=kLoop, calls=%fused_computation.2 | loop fusion | flops 1048576 | bytes 1048576 | tf_op jit(solution)/shard_map/concatenate | solution.py:147
  19.7 0.0 all-gather.2.cloned.1.call-update
  19.7 0.0 reduce-scatter.2.cloned.1.call-start
  19.8 0.8 copy.7
  20.5 0.1 pad_add_fusion
  20.6 0.6 broadcast_subtract_fusion.corner_ref
  21.2 22.6 %all-gather.2.cloned.1.call-done.ext_ref = bf16[2,1024,512]{2,1,0:T(8,128)(2,1)} async-done(((bf16[2,256,512]{2,1,0:T(8,128)(2,1)}), bf16[2,1024,512]{2,1,0:T(8,128)(2,1)}) %all-gather.2.cloned.1.call-update) | async-done | bytes 2097168 | tf_op jit(solution)/shard_map/all_gather | solution.py:146
  43.8 34.5 %shard_map.64 = f32[2,1024,512]{2,1,0:T(8,128)} custom-call(s32[4,2]{1,0:T(4,128)} %broadcast_subtract_fusion.corner_ref, bf16[2,1024,512]{2,1,0:T(8,128)(2,1)} %all-gather.2.cloned.1.call-done.ext_ref, f32[2,256,256]{2,1,0:T(8,128)} %illum_ref.1, f32[4,256,256]{2,1,0:T(8,128)} %meas_ref.1, bf16[4,512,512]{2,1,0:T(8,128)(2,1)} %constant.40.clone.high, ...), custom_call_target="tpu_custom_call" | custom-call | flops 12884901888 | bytes 16777216 | tf_op jit(solution)/shard_map/pallas_call | solution.py:128
  78.3 0.0 reduce-scatter.2.cloned.1.call-update
  78.3 44.7 %reduce-scatter.2.cloned.1.call-done = f32[2,256,512]{2,1,0:T(8,128)} async-done(((f32[2,1024,512]{2,1,0:T(8,128)}), f32[2,256,512]{2,1,0:T(8,128)}) %reduce-scatter.2.cloned.1.call-update) | async-done | bytes 1048592 | tf_op jit(solution)/shard_map/reduce_scatter | solution.py:160
  123.0 1.1 slice.9
  124.1 3.4 %collective-permute-start.1 = (f32[2,256,256]{2,1,0:T(8,128)S(1)}, f32[2,256,256]{2,1,0:T(8,128)S(1)}, u32[]{:S(2)}, u32[]{:S(2)}) collective-permute-start(f32[2,256,256]{2,1,0:T(8,128)S(1)} %slice.9), channel_id=1, source_target_pairs={{0,4},{4,8},{8,12},{12,16},{16,20},{20,24},{24,28},{1,5},{5,9},{9,... | collective-permute-start | bytes 1572872 | tf_op jit(solution)/shard_map/ppermute | solution.py:22
  127.5 11.2 %collective-permute-done.1 = f32[2,256,256]{2,1,0:T(8,128)S(1)} collective-permute-done((f32[2,256,256]{2,1,0:T(8,128)S(1)}, f32[2,256,256]{2,1,0:T(8,128)S(1)}, u32[]{:S(2)}, u32[]{:S(2)}) %collective-permute-start.1) | collective-permute-done | bytes 524320 | tf_op jit(solution)/shard_map/ppermute | solution.py:22
  138.6 1.9 %fusion = f32[2,1,256,256]{3,2,1,0:T(8,128)} fusion(f32[2,256,256]{2,1,0:T(8,128)S(1)} %collective-permute-done.1, f32[2,256,512]{2,1,0:T(8,128)} %reduce-scatter.2.cloned.1.call-done), kind=kLoop, calls=%fused_computation.1 | loop fusion | flops 131072 | bytes 1572864 | tf_op jit(solution)/shard_map/broadcast_in_dim | solution.py:163
Async XLA Ops:
  6.5 37.3 %all-gather.2.cloned.1.call-start = ((), (), s32[]{:S(2)}) async-start(), calls=%async_computation.1 | async-start | bytes 2621440 | tf_op jit(solution)/shard_map/all_gather | solution.py:146
  6.5 11.3 %collective-permute-start = (bf16[2,256,256]{2,1,0:T(8,128)(2,1)}, bf16[2,256,256]{2,1,0:T(8,128)(2,1)S(1)}, u32[]{:S(2)}, u32[]{:S(2)}) collective-permute-start(bf16[2,256,256]{2,1,0:T(8,128)(2,1)} %bitcast.7), channel_id=1, source_target_pairs={{4,0},{8,4},{12,8},{16,12},{20,16},{24,20},{28,24},{5,1},{9,5},{13... | collective-permute-start | bytes 786440 | tf_op jit(solution)/shard_map/ppermute | solution.py:22
  19.7 103.3 %reduce-scatter.2.cloned.1.call-start = ((), (), s32[]{:S(2)}) async-start(), calls=%async_computation.2 | async-start | bytes 5242880 | tf_op jit(solution)/shard_map/reduce_scatter | solution.py:160
  124.1 14.6 %collective-permute-start.1 = (f32[2,256,256]{2,1,0:T(8,128)S(1)}, f32[2,256,256]{2,1,0:T(8,128)S(1)}, u32[]{:S(2)}, u32[]{:S(2)}) collective-permute-start(f32[2,256,256]{2,1,0:T(8,128)S(1)} %slice.9), channel_id=1, source_target_pairs={{0,4},{4,8},{8,12},{12,16},{16,20},{20,24},{24,28},{1,5},{5,9},{9,... | collective-permute-start | bytes 1572872 | tf_op jit(solution)/shard_map/ppermute | solution.py:22
Sparse Core Ops, SparseCore 0:
  19.8 23.9 all-gather.1
  78.5 44.4 reduce-scatter.1
where the time goes:
time: 148 us; the launch traced here: 147 us
  waiting for transfers between devices  88.5 us (60%)
  Pallas kernels  34.5 us (23%)
  between operations  13.4 us (9%)
  starting transfers between devices  4.72 us (3%)
  other arithmetic  4.34 us (3%)
  local copies, waits for them, and re-layouts  1.84 us (1%)
    reduce_scatter x1, waiting for transfers between devices, body(): lax.psum_scatter(wide_grad, 'owner', scatter_dimension=1, tiled=True)  44.7 us
    pallas_call x1, Pallas kernels, probe_gradients(): pl.pallas_call(probes_kernel, out_shape=jax.ShapeDtypeStruct(extended.sha...  34.5 us
    all_gather x1, waiting for transfers between devices, body(): lax.all_gather(jnp.concatenate([rows_part, right_rim], axis=2), 'owner',...  22.6 us
    ppermute x2, waiting for transfers between devices, passed_along(): return lax.ppermute(block, axis, route)  21.2 us
    ppermute x2, starting transfers between devices, passed_along(): return lax.ppermute(block, axis, route)  4.67 us
  transfers between devices with their start and end apart: 4, of which 4 were waited for; matrix products, arithmetic and copies ran while one was open for 1% of the time, Pallas kernels for 0%

commit v1 on v0

--- a/solution.py
+++ b/solution.py
@@ -14,6 +14,7 @@
 SIGMA = 0.5
 LOSS_WEIGHT = 0.125
 ALIGN = 16
+MESH = pl.DeviceIdType.MESH
 
 
 def passed_along(block, axis, distance):
@@ -136,16 +137,226 @@
     )(corners, extended, illumination, measured, jnp.asarray(high), jnp.asarray(low))
 
 
+def places():
+    tile, owner = lax.axis_index("tile"), lax.axis_index("owner")
+    partner = owner + 1 - 2 * (owner % 2)
+    return tile, owner, partner, tile % TX != 0, tile % TX != TX - 1
+
+
+def greet(owners):
+    tile, owner, partner, has_left, has_right = places()
+    barrier = pltpu.get_barrier_semaphore()
+
+    def hello(device):
+        pl.semaphore_signal(barrier, inc=1, device_id=device, device_id_type=MESH)
+
+    hello({"owner": partner})
+    for j in range(1, owners // 2):
+        hello({"owner": (owner + 2 * j) % owners})
+    pl.when(has_left)(lambda: hello({"tile": tile - 1}))
+    pl.when(has_right)(lambda: hello({"tile": tile + 1}))
+    beside = has_left.astype(jnp.int32) + has_right.astype(jnp.int32)
+    pl.semaphore_wait(barrier, owners // 2 + beside)
+
+
+def gather_kernel(owners, part_ref, ext_ref, send, recv):
+    tile, owner, partner, has_left, has_right = places()
+    layers, size, width = part_ref.shape
+    chips = owners // 2
+    peers = range(1, chips)
+
+    def spot(s, who, side):
+        start = pl.multiple_of(who * size, size)
+        return ext_ref.at[s, pl.ds(start, size), pl.ds(side * width, width)]
+
+    def copy(s, kind, src, dst, device):
+        return pltpu.make_async_remote_copy(
+            src_ref=src, dst_ref=dst, send_sem=send.at[s, kind], recv_sem=recv.at[s, kind],
+            device_id=device, device_id_type=MESH,
+        )
+
+    def to_left(s):
+        return copy(s, 0, part_ref.at[s], spot(s, owner, 1), {"tile": tile - 1})
+
+    def to_partner(s, side):
+        src = part_ref.at[s] if side == 0 else spot(s, owner, 1)
+        return copy(s, 1 + side, src, spot(s, owner, side), {"owner": partner})
+
+    def to_peer(s, side, j):
+        src = part_ref.at[s] if side == 0 else spot(s, owner, 1)
+        kind = 3 + side * (chips - 1) + j - 1
+        return copy(s, kind, src, spot(s, owner, side), {"owner": (owner + 2 * j) % owners})
+
+    def onward(s, side, j):
+        block = spot(s, (owner + owners - 2 * j) % owners, side)
+        kind = 3 + (2 + side) * (chips - 1) + j - 1
+        return copy(s, kind, block, block, {"owner": partner})
+
+    greet(owners)
+
+    def spread(s, side):
+        for j in peers:
+            to_peer(s, side, j).start()
+        to_partner(s, side).start()
+
+    def pass_on(s, side):
+        for j in peers:
+            to_peer(s, side, j).wait_recv()
+            onward(s, side, j).start()
+
+    def finish(s, side):
+        to_partner(s, side).wait()
+        for j in peers:
+            to_peer(s, side, j).wait_send()
+            onward(s, side, j).wait()
+
+    for s in range(layers):
+        pl.when(has_left)(lambda s=s: to_left(s).start())
+    spread(0, 0)
+    for s in range(layers):
+        @pl.when(has_right)
+        def _(s=s):
+            to_left(s).wait_recv()
+            spread(s, 1)
+
+        if s + 1 < layers:
+            spread(s + 1, 0)
+        ext_ref[s, pl.ds(pl.multiple_of(owner * size, size), size), :width] = part_ref[s]
+
+        @pl.when(jnp.logical_not(has_right))
+        def _(s=s):
+            ext_ref[s, :, width:] = jnp.zeros((ext_ref.shape[1], width), ext_ref.dtype)
+
+    for s in range(layers):
+        pass_on(s, 0)
+        pl.when(has_right)(lambda s=s: pass_on(s, 1))
+    for s in range(layers):
+        finish(s, 0)
+        pl.when(has_right)(lambda s=s: finish(s, 1))
+        pl.when(has_left)(lambda s=s: to_left(s).wait_send())
+
+
+def gather_grid(rows_part):
+    owners = lax.axis_size("owner")
+    layers, size, width = rows_part.shape
+    kinds = 3 + 4 * (owners // 2 - 1)
+    vmem = pl.BlockSpec(memory_space=pltpu.VMEM)
+    return pl.pallas_call(
+        functools.partial(gather_kernel, owners),
+        out_shape=jax.ShapeDtypeStruct((layers, owners * size, 2 * width), rows_part.dtype),
+        in_specs=[vmem],
+        out_specs=vmem,
+        scratch_shapes=[pltpu.SemaphoreType.DMA((layers, kinds))] * 2,
+        compiler_params=pltpu.CompilerParams(
+            collective_id=0, has_side_effects=True, vmem_limit_bytes=56 * 2**20
+        ),
+    )(rows_part)
+
+
+def reduce_kernel(owners, grad_ref, out_ref, near, total, far, edge, edge_in, sends, recvs):
+    tile, owner, partner, has_left, has_right = places()
+    layers, size, width = out_ref.shape
+    chips = owners // 2
+    order = [(s, side) for side in (1, 0) for s in range(layers)]
+
+    def rows(who):
+        return pl.ds(pl.multiple_of(who * size, size), size)
+
+    def cols(side):
+        return pl.ds(side * width, width)
+
+    def to_partner(s, side, j):
+        src = grad_ref.at[s, rows((partner + 2 * j) % owners), cols(side)]
+        return pltpu.make_async_remote_copy(
+            src_ref=src, dst_ref=near.at[s, side, j],
+            send_sem=sends.at[s, side, j], recv_sem=recvs.at[s, side, j],
+            device_id={"owner": partner}, device_id_type=MESH,
+        )
+
+    def to_peer(s, side, j):
+        return pltpu.make_async_remote_copy(
+            src_ref=total.at[s, side, j - 1], dst_ref=far.at[s, side, j - 1],
+            send_sem=sends.at[s, side, chips + j - 1], recv_sem=recvs.at[s, side, chips + j - 1],
+            device_id={"owner": (owner + 2 * j) % owners}, device_id_type=MESH,
+        )
+
+    def to_right(s):
+        return pltpu.make_async_remote_copy(
+            src_ref=edge.at[s], dst_ref=edge_in.at[s],
+            send_sem=sends.at[s, 0, 2 * chips - 1], recv_sem=recvs.at[s, 0, 2 * chips - 1],
+            device_id={"tile": tile + 1}, device_id_type=MESH,
+        )
+
+    greet(owners)
+    peers = list(range(1, chips))
+    for s, side in order:
+        for j in peers + [0]:
+            to_partner(s, side, j).start()
+    for s, side in order:
+        for j in peers:
+            to_partner(s, side, j).wait_recv()
+            own = grad_ref[s, rows((owner + 2 * j) % owners), cols(side)]
+            total[s, side, j - 1] = own + near[s, side, j]
+            to_peer(s, side, j).start()
+    for s, side in order:
+        to_partner(s, side, 0).wait_recv()
+        value = grad_ref[s, rows(owner), cols(side)] + near[s, side, 0]
+        for j in peers:
+            to_peer(s, side, j).wait_recv()
+            value = value + far[s, side, j - 1]
+        if side == 1:
+            edge[s] = value
+            pl.when(has_right)(lambda s=s: to_right(s).start())
+        else:
+            out_ref[s] = value
+    for s in range(layers):
+        @pl.when(has_left)
+        def _(s=s):
+            to_right(s).wait_recv()
+            out_ref[s] += edge_in[s]
+
+    for s, side in order:
+        for j in peers + [0]:
+            to_partner(s, side, j).wait_send()
+        for j in peers:
+            to_peer(s, side, j).wait_send()
+    for s in range(layers):
+        pl.when(has_right)(lambda s=s: to_right(s).wait_send())
+
+
+def reduce_grid(wide_grad):
+    owners = lax.axis_size("owner")
+    layers, tile_rows, cols = wide_grad.shape
+    size, width, chips = tile_rows // owners, cols // 2, owners // 2
+    vmem = pl.BlockSpec(memory_space=pltpu.VMEM)
+    block = (size, width)
+    return pl.pallas_call(
+        functools.partial(reduce_kernel, owners),
+        out_shape=jax.ShapeDtypeStruct((layers,) + block, jnp.float32),
+        in_specs=[vmem],
+        out_specs=vmem,
+        scratch_shapes=[
+            pltpu.VMEM((layers, 2, chips) + block, jnp.float32),
+            pltpu.VMEM((layers, 2, max(chips - 1, 1)) + block, jnp.float32),
+            pltpu.VMEM((layers, 2, max(chips - 1, 1)) + block, jnp.float32),
+            pltpu.VMEM((layers,) + block, jnp.float32),
+            pltpu.VMEM((layers,) + block, jnp.float32),
+            pltpu.SemaphoreType.DMA((layers, 2, 2 * chips)),
+            pltpu.SemaphoreType.DMA((layers, 2, 2 * chips)),
+        ],
+        compiler_params=pltpu.CompilerParams(
+            collective_id=1, has_side_effects=True, vmem_limit_bytes=56 * 2**20
+        ),
+    )(wide_grad)
+
+
 def body(potential, positions, illumination, measured):
     probe_width = illumination.shape[1]
     rows_part = potential[:, 0]
     tile_rows = rows_part.shape[1] * lax.axis_size("owner")
     tile_cols = rows_part.shape[2]
     below = lax.axis_size("tile") > TX
-    right_rim = passed_along(rows_part, "tile", -1)
-    extended = lax.all_gather(
-        jnp.concatenate([rows_part, right_rim], axis=2), "owner", axis=1, tiled=True
-    )
+    extended = gather_grid(rows_part)
     if below:
         lower_rim = passed_along(extended[:, :probe_width, :], "tile", -TX)
         extended = jnp.concatenate([extended, lower_rim], axis=1)
@@ -157,10 +368,7 @@
     if below:
         upper_back = passed_along(accumulated[:, tile_rows:, :], "tile", TX)
         wide_grad = wide_grad.at[:, :probe_width, :].add(upper_back)
-    row_shard = lax.psum_scatter(wide_grad, "owner", scatter_dimension=1, tiled=True)
-    left_back = passed_along(row_shard[:, :, tile_cols:], "tile", 1)
-    result = row_shard[:, :, :tile_cols] + left_back
-    return result[:, None]
+    return reduce_grid(wide_grad)[:, None]
 
 
 def solution(mesh):

time: 148 us -> 89.3 us (0.60)
  waiting for transfers between devices: 88.5 us -> 0 us
  Pallas kernels: 34.5 us -> 85.7 us
  between operations: 13.4 us -> 0.02 us
  starting transfers between devices: 4.72 us -> 0 us
  other arithmetic: 4.34 us -> 0.66 us
    pallas_call x0 -> x2, Pallas kernels: none -> 51.2 us  [the longest x1 30.2 us: reduce_grid(): pl.pallas_call(functools.partial(reduce_kernel, owners), out_shape=jax.Sh...]
    reduce_scatter x1 -> x0, waiting for transfers between devices: 44.7 us -> none  [body(): lax.psum_scatter(wide_grad, 'owner', scatter_dimension=1, tiled=True)]
    all_gather x1 -> x0, waiting for transfers between devices: 22.6 us -> none  [body(): lax.all_gather(jnp.concatenate([rows_part, right_rim], axis=2), 'owner',...]
    ppermute x2 -> x0, waiting for transfers between devices: 21.2 us -> none  [passed_along(): return lax.ppermute(block, axis, route)]
    ppermute x2 -> x0, starting transfers between devices: 4.67 us -> none  [passed_along(): return lax.ppermute(block, axis, route)]
    broadcast_in_dim x1 -> x0, other arithmetic: 1.9 us -> none  [body(): return result[:, None]]
    unnamed x1 -> x2, local copies, waits for them, and re-layouts: 0.77 us -> 2.63 us
    concatenate x1 -> x0, other arithmetic: 1.78 us -> none  [body(): jnp.concatenate([rows_part, right_rim], axis=2)]
  transfers between devices with their start and end apart: 4 -> 0, of which waited for: 4 -> 0; matrix products, arithmetic and copies ran while one was open for 1% -> 0% of each run, Pallas kernels for 0% -> 0%
where the time goes in v1:
time: 89.3 us; the launch traced here: 89 us
  Pallas kernels  85.7 us (96%)
  local copies, waits for them, and re-layouts  2.63 us (3%)
    pallas_call x1, Pallas kernels, probe_gradients(): pl.pallas_call(probes_kernel, out_shape=jax.ShapeDtypeStruct(extended.sha...  34.5 us
    pallas_call x1, Pallas kernels, reduce_grid(): pl.pallas_call(functools.partial(reduce_kernel, owners), out_shape=jax.Sh...  30.2 us
    pallas_call x1, Pallas kernels, gather_grid(): pl.pallas_call(functools.partial(gather_kernel, owners), out_shape=jax.Sh...  21 us
    unnamed x2, local copies, waits for them, and re-layouts  2.63 us

profile of v1, /device:TPU:0, one launch (start us, length us, event | category | flops | bytes accessed | tf_op | source)
XLA Modules:
  0.0 89.0 jit_solution(9342585991393617130)
XLA Ops:
  0.0 0.1 pad_add_fusion
  0.1 0.8 copy.7
  0.8 0.6 broadcast_subtract_fusion.corner_ref
  1.4 21.0 %shard_map.64.ext_ref = bf16[2,1024,512]{2,1,0:T(8,128)(2,1)} custom-call(bf16[2,256,256]{2,1,0:T(8,128)(2,1)} %bitcast.7), custom_call_target="tpu_custom_call" | custom-call | tf_op jit(solution)/shard_map/pallas_call | solution.py:244
  22.4 34.5 %shard_map.65.grad_ref = f32[2,1024,512]{2,1,0:T(8,128)} custom-call(s32[4,2]{1,0:T(4,128)} %broadcast_subtract_fusion.corner_ref, bf16[2,1024,512]{2,1,0:T(8,128)(2,1)} %shard_map.64.ext_ref, f32[2,256,256]{2,1,0:T(8,128)} %illum_ref.1, f32[4,256,256]{2,1,0:T(8,128)} %meas_ref.1, bf16[4,512,512]{2,1,0:T(8,128)(2,1)} %constant.40.clone.high, ...), custom_call_target="tpu_custom_call" | custom-call | flops 12884901888 | bytes 16777216 | tf_op jit(solution)/shard_map/pallas_call | solution.py:129
  56.9 30.2 %shard_map.66 = f32[2,256,256]{2,1,0:T(8,128)} custom-call(f32[2,1024,512]{2,1,0:T(8,128)} %shard_map.65.grad_ref), custom_call_target="tpu_custom_call" | custom-call | tf_op jit(solution)/shard_map/pallas_call | solution.py:333
  87.2 1.9 %copy.10 = f32[2,1,256,256]{3,2,1,0:T(8,128)} copy(f32[2,1,256,256]{3,2,1,0:T(8,128)} %bitcast.6) | data formatting | bytes 1048576

commit v2 on v1

--- a/solution.py
+++ b/solution.py
@@ -350,12 +350,313 @@
     )(wide_grad)
 
 
+def fused_kernel(
+    owners, place_ref, part_ref, illum_ref, meas_hbm, high_hbm, low_hbm, out_ref,
+    ext0, ext1, meas_ref, high, low, first, back, pads, grad, near, total, far, edge, edge_in,
+    loads, g_send, g_recv, sends, recvs,
+):
+    tile, owner, partner, has_left, has_right = places()
+    layers, groups, _, width = part_ref.shape
+    size = groups * ALIGN
+    chips = owners // 2
+    peers = list(range(1, chips))
+    probes = meas_ref.shape[0]
+    cols_all = 2 * width
+    rows_all = owners * size
+    span = width + ALIGN
+    ext = (ext0, ext1)
+    tail = width + 8
+
+    fetches = [
+        pltpu.make_async_copy(src, dst, loads.at[i])
+        for i, (src, dst) in enumerate(((high_hbm, high), (low_hbm, low), (meas_hbm, meas_ref)))
+    ]
+    for fetch in fetches:
+        fetch.start()
+    greet(owners)
+
+    def spot(s, who, side):
+        return ext[s].at[pl.ds(who * groups, groups), :, pl.ds(side * width, width)]
+
+    def g_copy(s, kind, src, dst, device):
+        return pltpu.make_async_remote_copy(
+            src_ref=src, dst_ref=dst, send_sem=g_send.at[s, kind], recv_sem=g_recv.at[s, kind],
+            device_id=device, device_id_type=MESH,
+        )
+
+    def own(s, side):
+        return part_ref.at[s] if side == 0 else spot(s, owner, 1)
+
+    def g_left(s):
+        return g_copy(s, 0, part_ref.at[s], spot(s, owner, 1), {"tile": tile - 1})
+
+    def g_partner(s, side):
+        return g_copy(s, 1 + side, own(s, side), spot(s, owner, side), {"owner": partner})
+
+    def g_peer(s, side, j):
+        kind = 3 + side * (chips - 1) + j - 1
+        device = {"owner": (owner + 2 * j) % owners}
+        return g_copy(s, kind, own(s, side), spot(s, owner, side), device)
+
+    def g_onward(s, side, j):
+        block = spot(s, (owner + owners - 2 * j) % owners, side)
+        kind = 3 + (2 + side) * (chips - 1) + j - 1
+        return g_copy(s, kind, block, block, {"owner": partner})
+
+    def spread(s, side):
+        for j in peers:
+            g_peer(s, side, j).start()
+        g_partner(s, side).start()
+
+    def pass_on(s, side):
+        for j in peers:
+            g_peer(s, side, j).wait_recv()
+            g_onward(s, side, j).start()
+
+    def landed(s, side):
+        g_partner(s, side).wait_recv()
+        for j in peers:
+            g_onward(s, side, j).wait_recv()
+
+    def sent(s, side):
+        g_partner(s, side).wait_send()
+        for j in peers:
+            g_peer(s, side, j).wait_send()
+            g_onward(s, side, j).wait_send()
+
+    def right_spread(s):
+        g_left(s).wait_recv()
+        spread(s, 1)
+
+    for s in range(layers):
+        pl.when(has_left)(lambda s=s: g_left(s).start())
+    spread(0, 0)
+    blank = jnp.zeros((probes, size // 8, 8, cols_all), jnp.float32)
+    pads[:, : size // 8] = blank
+    pads[:, (size + tail) // 8 :] = blank
+    for s in range(layers):
+        ext[s][pl.ds(owner * groups, groups), :, :width] = part_ref[s]
+
+        @pl.when(jnp.logical_not(has_right))
+        def _(s=s):
+            ext[s][:, :, width:] = jnp.zeros((rows_all // ALIGN, ALIGN, width), part_ref.dtype)
+
+    pl.when(has_right)(lambda: right_spread(0))
+    spread(1, 0)
+    pass_on(0, 0)
+    pl.when(has_right)(lambda: pass_on(0, 1))
+    pl.when(has_right)(lambda: right_spread(1))
+    pass_on(1, 0)
+    pl.when(has_right)(lambda: pass_on(1, 1))
+    for s in range(layers):
+        landed(s, 0)
+        pl.when(has_right)(lambda s=s: landed(s, 1))
+    for fetch in fetches:
+        fetch.wait()
+
+    def pick(shape, dim, shift):
+        along = lax.broadcasted_iota(jnp.int32, shape, dim)
+        other = lax.broadcasted_iota(jnp.int32, shape, 1 - dim)
+        return jnp.where(along == other + shift, 1.0, 0.0).astype(jnp.bfloat16)
+
+    def dot(x, y):
+        return jnp.dot(x, y, preferred_element_type=jnp.float32)
+
+    def cut(s, p):
+        base = place_ref[p, 0]
+        x = jnp.concatenate([ext[s][base + i] for i in range(span // ALIGN)], axis=0)
+        x = dot(x, pick((cols_all, width), 0, place_ref[p, 2])).astype(jnp.bfloat16)
+        return dot(pick((width, span), 1, place_ref[p, 1]), x)
+
+    def paste(p, g):
+        down = pick((tail, width), 0, place_ref[p, 3])
+        a, b = halves(g)
+        a, b = halves(dot(down, a) + dot(down, b))
+        along = pick((width, cols_all), 1, place_ref[p, 2])
+        value = dot(a, along) + dot(b, along)
+        pads[p, pl.ds(size // 8, tail // 8)] = value.reshape(tail // 8, 8, cols_all)
+
+    def forward(p, carry):
+        cos0, sin0 = turn(cut(0, p))
+        first_r = illum_ref[0] * cos0 - illum_ref[1] * sin0
+        first_i = illum_ref[0] * sin0 + illum_ref[1] * cos0
+        first[p, 0] = first_r
+        first[p, 1] = first_i
+        mid_r, mid_i = both_sides(first_r, first_i, high, low, 2)
+        cos1, sin1 = turn(cut(1, p))
+        exit_r = mid_r * cos1 - mid_i * sin1
+        exit_i = mid_r * sin1 + mid_i * cos1
+        far_r, far_i = both_sides(exit_r, exit_i, high, low, 0)
+        misfit = far_r * far_r + far_i * far_i - meas_ref[p]
+        scale = (4.0 * LOSS_WEIGHT) * misfit
+        g_r, g_i = both_sides(scale * far_r, scale * far_i, high, low, 1)
+        paste(p, SIGMA * (g_i * exit_r - g_r * exit_i))
+        back[p, 0] = g_r * cos1 + g_i * sin1
+        back[p, 1] = g_i * cos1 - g_r * sin1
+        return carry
+
+    def backward(p, carry):
+        g_r, g_i = both_sides(back[p, 0], back[p, 1], high, low, 3)
+        paste(p, SIGMA * (g_i * first[p, 0] - g_r * first[p, 1]))
+        return carry
+
+    def rows(who):
+        return pl.ds(pl.multiple_of(who * size, size), size)
+
+    def cols(side):
+        return pl.ds(side * width, width)
+
+    def r_copy(s, kind, src, dst, device):
+        return pltpu.make_async_remote_copy(
+            src_ref=src, dst_ref=dst, send_sem=sends.at[s, kind], recv_sem=recvs.at[s, kind],
+            device_id=device, device_id_type=MESH,
+        )
+
+    def to_partner(s, side, j):
+        src = grad.at[s, rows((partner + 2 * j) % owners), cols(side)]
+        return r_copy(s, side * chips + j, src, near.at[s, side, j], {"owner": partner})
+
+    def to_peer(s, side, j):
+        kind = 2 * chips + side * (chips - 1) + j - 1
+        device = {"owner": (owner + 2 * j) % owners}
+        return r_copy(s, kind, total.at[s, side, j - 1], far.at[s, side, j - 1], device)
+
+    def to_right(s):
+        return r_copy(s, 4 * chips - 2, edge.at[s], edge_in.at[s], {"tile": tile + 1})
+
+    def block_sum(who, side):
+        starts = [place_ref[p, 4 + who] for p in range(probes)]
+        parts = []
+        for i in range(size // 8):
+            terms = [pads[p, starts[p] + i, :, cols(side)] for p in range(probes)]
+            parts.append(functools.reduce(jnp.add, terms))
+        value = jnp.concatenate(parts, axis=0)
+        return value
+
+    def give(s):
+        for side in (1, 0):
+            for j in peers + [0]:
+                who = (partner + 2 * j) % owners
+                grad[s, rows(who), cols(side)] = block_sum(who, side)
+                to_partner(s, side, j).start()
+        for side in (1, 0):
+            for j in peers + [0]:
+                who = (owner + 2 * j) % owners
+                grad[s, rows(who), cols(side)] = block_sum(who, side)
+
+    def across(s):
+        for side in (1, 0):
+            for j in peers:
+                to_partner(s, side, j).wait_recv()
+                mine = grad[s, rows((owner + 2 * j) % owners), cols(side)]
+                total[s, side, j - 1] = mine + near[s, side, j]
+                to_peer(s, side, j).start()
+
+    def collect(s, side):
+        to_partner(s, side, 0).wait_recv()
+        value = grad[s, rows(owner), cols(side)] + near[s, side, 0]
+        for j in peers:
+            to_peer(s, side, j).wait_recv()
+            value = value + far[s, side, j - 1]
+        if side == 1:
+            edge[s] = value
+            pl.when(has_right)(lambda: to_right(s).start())
+        else:
+            out_ref[s] = value
+
+    def add_edge(s):
+        to_right(s).wait_recv()
+        out_ref[s] += edge_in[s]
+
+    lax.fori_loop(0, probes, forward, 0)
+    give(1)
+    lax.fori_loop(0, 1, backward, 0)
+    across(1)
+    lax.fori_loop(1, probes, backward, 0)
+    give(0)
+    across(0)
+    for side in (1, 0):
+        for s in (1, 0):
+            collect(s, side)
+    for s in (1, 0):
+        pl.when(has_left)(lambda s=s: add_edge(s))
+
+    for s in range(layers):
+        sent(s, 0)
+        pl.when(has_right)(lambda s=s: sent(s, 1))
+        pl.when(has_left)(lambda s=s: g_left(s).wait_send())
+        for side in (0, 1):
+            for j in peers + [0]:
+                to_partner(s, side, j).wait_send()
+            for j in peers:
+                to_peer(s, side, j).wait_send()
+        pl.when(has_right)(lambda s=s: to_right(s).wait_send())
+
+
+def fused(rows_part, positions, illumination, measured):
+    owners = lax.axis_size("owner")
+    layers, size, width = rows_part.shape
+    probes = measured.shape[0]
+    chips = owners // 2
+    peers = max(chips - 1, 1)
+    high, low = block_tables(width)
+    tile = lax.axis_index("tile")
+    row = positions[:, 0] - tile // TX * (owners * size)
+    col = positions[:, 1] - tile % TX * width
+    base = jnp.minimum(row // ALIGN * ALIGN, owners * size - width - ALIGN)
+    starts = size + jnp.arange(owners)[None, :] * size - (row // 8 * 8)[:, None]
+    starts = jnp.clip(starts, 0, size + width + 8)
+    heads = jnp.stack([base // ALIGN, row - base, col, row % 8], axis=1)
+    place = jnp.concatenate([heads, starts // 8], axis=1)
+    place = place.astype(jnp.int32)
+    grouped = rows_part.reshape(layers, size // ALIGN, ALIGN, width)
+    vmem = pl.BlockSpec(memory_space=pltpu.VMEM)
+    anywhere = pl.BlockSpec(memory_space=pl.ANY)
+    block = (size, width)
+    f32 = jnp.float32
+    flops = probes * 4 * 2 * 3 * 2 * (2 * width) ** 2 * width
+    return pl.pallas_call(
+        functools.partial(fused_kernel, owners),
+        out_shape=jax.ShapeDtypeStruct((layers,) + block, f32),
+        in_specs=[pl.BlockSpec(memory_space=pltpu.SMEM), vmem, vmem] + [anywhere] * 3,
+        out_specs=vmem,
+        scratch_shapes=[
+            pltpu.VMEM((owners * size // ALIGN, ALIGN, 2 * width), rows_part.dtype),
+            pltpu.VMEM((owners * size // ALIGN, ALIGN, 2 * width), rows_part.dtype),
+            pltpu.VMEM(measured.shape, f32),
+            pltpu.VMEM(high.shape, jnp.bfloat16),
+            pltpu.VMEM(low.shape, jnp.bfloat16),
+            pltpu.VMEM((probes, 2, width, width), f32),
+            pltpu.VMEM((probes, 2, width, width), f32),
+            pltpu.VMEM((probes, (2 * size + width) // 8 + 1, 8, 2 * width), f32),
+            pltpu.VMEM((layers, owners * size, 2 * width), f32),
+            pltpu.VMEM((layers, 2, chips) + block, f32),
+            pltpu.VMEM((layers, 2, peers) + block, f32),
+            pltpu.VMEM((layers, 2, peers) + block, f32),
+            pltpu.VMEM((layers,) + block, f32),
+            pltpu.VMEM((layers,) + block, f32),
+            pltpu.SemaphoreType.DMA((3,)),
+            pltpu.SemaphoreType.DMA((layers, 3 + 4 * (chips - 1))),
+            pltpu.SemaphoreType.DMA((layers, 3 + 4 * (chips - 1))),
+            pltpu.SemaphoreType.DMA((layers, 4 * chips - 1)),
+            pltpu.SemaphoreType.DMA((layers, 4 * chips - 1)),
+        ],
+        compiler_params=pltpu.CompilerParams(
+            collective_id=2, has_side_effects=True, vmem_limit_bytes=56 * 2**20
+        ),
+        cost_estimate=pl.CostEstimate(flops=flops, bytes_accessed=8 * 2**20, transcendentals=0),
+    )(place, grouped, illumination, measured, jnp.asarray(high), jnp.asarray(low))
+
+
 def body(potential, positions, illumination, measured):
     probe_width = illumination.shape[1]
     rows_part = potential[:, 0]
+    layers = rows_part.shape[0]
     tile_rows = rows_part.shape[1] * lax.axis_size("owner")
     tile_cols = rows_part.shape[2]
     below = lax.axis_size("tile") > TX
+    if not below and layers == 2:
+        return fused(rows_part, positions, illumination, measured)[:, None]
     extended = gather_grid(rows_part)
     if below:
         lower_rim = passed_along(extended[:, :probe_width, :], "tile", -TX)

time: 89.3 us -> 78.7 us (0.88); the launches traced: 89 us -> 77.5 us
  Pallas kernels: 85.7 us -> 73.8 us
    pallas_call x3 -> x1, Pallas kernels: 85.7 us -> 73.8 us  [fused(): pl.pallas_call(functools.partial(fused_kernel, owners), out_shape=jax.Sha...]
    unnamed x2 -> x3, local copies, waits for them, and re-layouts: 2.63 us -> 2.06 us
where the time goes in v2:
time: 78.7 us; the launch traced here: 77.5 us
  Pallas kernels  73.8 us (94%)
  local copies, waits for them, and re-layouts  3.48 us (4%)
    pallas_call x1, Pallas kernels, fused(): pl.pallas_call(functools.partial(fused_kernel, owners), out_shape=jax.Sha...  73.8 us
    unnamed x3, local copies, waits for them, and re-layouts  2.06 us

profile of v2, /device:TPU:0, one launch (start us, length us, event | category | flops | bytes accessed | tf_op | source)
XLA Modules:
  0.0 77.5 jit_solution(13445943182844364389)
XLA Ops:
  0.0 0.8 fusion.10
  0.8 0.1 copy.14
  0.9 0.1 copy.13
  0.9 0.1 fusion.5
  1.1 0.1 add_select_fusion
  1.2 0.7 concatenate.3.place_ref
  1.8 73.8 %shard_map.64 = f32[2,256,256]{2,1,0:T(8,128)} custom-call(s32[4,8]{1,0:T(4,128)} %concatenate.3.place_ref, bf16[2,16,16,256]{3,2,1,0:T(8,128)(2,1)} %bitcast.5, f32[2,256,256]{2,1,0:T(8,128)} %illum_ref.1, f32[4,256,256]{2,1,0:T(8,128)} %meas_hbm.1, bf16[4,512,512]{2,1,0:T(8,128)(2,1)} %constant.93.clone.high_hbm, bf16[4,512,512]{2,1,0:T(8,128)(2,1)} %constant.94.clone.low_hbm), custom_call_target="tpu_custom_call" | custom-call | flops 12884901888 | bytes 8388608 | tf_op jit(solution)/shard_map/pallas_call | solution.py:618
  75.6 1.9 %copy.16 = f32[2,1,256,256]{3,2,1,0:T(8,128)} copy(f32[2,1,256,256]{3,2,1,0:T(8,128)} %bitcast.4) | data formatting | bytes 1048576
  (1 shorter events, 0.0 us)

commit v3 on v2

--- a/solution.py
+++ b/solution.py
@@ -14,6 +14,7 @@
 SIGMA = 0.5
 LOSS_WEIGHT = 0.125
 ALIGN = 16
+GROUP = 2
 MESH = pl.DeviceIdType.MESH
 
 
@@ -62,6 +63,19 @@
     other = which ^ 1
     tall = dot3((high[other], low[other]), halves(tall))
     return tall[:width], tall[width:]
+
+
+def both_sides_of(waves, high, low, which):
+    width = waves[0][0].shape[0]
+    wide = jnp.concatenate([jnp.concatenate(wave, axis=1) for wave in waves], axis=0)
+    wide = dot3(halves(wide), (high[which], low[which]))
+    spans = [slice(k * width, (k + 1) * width) for k in range(len(waves))]
+    real = jnp.concatenate([wide[span, :width] for span in spans], axis=1)
+    imag = jnp.concatenate([wide[span, width:] for span in spans], axis=1)
+    tall = jnp.concatenate([real, imag], axis=0)
+    other = which ^ 1
+    tall = dot3((high[other], low[other]), halves(tall))
+    return [(tall[:width, span], tall[width:, span]) for span in spans]
 
 
 def turn(window):
@@ -350,10 +364,37 @@
     )(wide_grad)
 
 
+def encode(x):
+    largest = jnp.maximum(jnp.max(jnp.abs(x), axis=0, keepdims=True), 1e-30)
+    code = jnp.round(x * (32767.0 / largest)).astype(jnp.int32).astype(jnp.int16)
+    return code, jnp.broadcast_to(largest * (1.0 / 32767.0), (8, x.shape[1]))
+
+
+def decode(code, scale):
+    return code.astype(jnp.int32).astype(jnp.float32) * scale[:1]
+
+
+class Several:
+    def __init__(self, *copies):
+        self.copies = copies
+
+    def start(self):
+        for copy in self.copies:
+            copy.start()
+
+    def wait_send(self):
+        for copy in self.copies:
+            copy.wait_send()
+
+    def wait_recv(self):
+        for copy in self.copies:
+            copy.wait_recv()
+
+
 def fused_kernel(
     owners, place_ref, part_ref, illum_ref, meas_hbm, high_hbm, low_hbm, out_ref,
     ext0, ext1, meas_ref, high, low, first, back, pads, grad, near, total, far, edge, edge_in,
-    loads, g_send, g_recv, sends, recvs,
+    total_scale, far_scale, edge_scale, edge_in_scale, loads, g_send, g_recv, sends, recvs,
 ):
     tile, owner, partner, has_left, has_right = places()
     layers, groups, _, width = part_ref.shape
@@ -446,11 +487,8 @@
     pass_on(0, 0)
     pl.when(has_right)(lambda: pass_on(0, 1))
     pl.when(has_right)(lambda: right_spread(1))
-    pass_on(1, 0)
-    pl.when(has_right)(lambda: pass_on(1, 1))
-    for s in range(layers):
-        landed(s, 0)
-        pl.when(has_right)(lambda s=s: landed(s, 1))
+    landed(0, 0)
+    pl.when(has_right)(lambda: landed(0, 1))
     for fetch in fetches:
         fetch.wait()
 
@@ -476,28 +514,45 @@
         value = dot(a, along) + dot(b, along)
         pads[p, pl.ds(size // 8, tail // 8)] = value.reshape(tail // 8, 8, cols_all)
 
-    def forward(p, carry):
-        cos0, sin0 = turn(cut(0, p))
-        first_r = illum_ref[0] * cos0 - illum_ref[1] * sin0
-        first_i = illum_ref[0] * sin0 + illum_ref[1] * cos0
-        first[p, 0] = first_r
-        first[p, 1] = first_i
-        mid_r, mid_i = both_sides(first_r, first_i, high, low, 2)
-        cos1, sin1 = turn(cut(1, p))
-        exit_r = mid_r * cos1 - mid_i * sin1
-        exit_i = mid_r * sin1 + mid_i * cos1
-        far_r, far_i = both_sides(exit_r, exit_i, high, low, 0)
-        misfit = far_r * far_r + far_i * far_i - meas_ref[p]
-        scale = (4.0 * LOSS_WEIGHT) * misfit
-        g_r, g_i = both_sides(scale * far_r, scale * far_i, high, low, 1)
-        paste(p, SIGMA * (g_i * exit_r - g_r * exit_i))
-        back[p, 0] = g_r * cos1 + g_i * sin1
-        back[p, 1] = g_i * cos1 - g_r * sin1
+    def members(g):
+        return [g * GROUP + k for k in range(GROUP)]
+
+    def enter(g, carry):
+        waves = []
+        for p in members(g):
+            cos0, sin0 = turn(cut(0, p))
+            first[p, 0] = illum_ref[0] * cos0 - illum_ref[1] * sin0
+            first[p, 1] = illum_ref[0] * sin0 + illum_ref[1] * cos0
+            waves.append((first[p, 0], first[p, 1]))
+        waves = both_sides_of(waves, high, low, 2)
+        for p, (real, imag) in zip(members(g), waves):
+            back[p, 0] = real
+            back[p, 1] = imag
         return carry
 
-    def backward(p, carry):
-        g_r, g_i = both_sides(back[p, 0], back[p, 1], high, low, 3)
-        paste(p, SIGMA * (g_i * first[p, 0] - g_r * first[p, 1]))
+    def forward(g, carry):
+        turns, exits = [], []
+        for p in members(g):
+            cos1, sin1 = turn(cut(1, p))
+            mid_r, mid_i = back[p, 0], back[p, 1]
+            turns.append((cos1, sin1))
+            exits.append((mid_r * cos1 - mid_i * sin1, mid_r * sin1 + mid_i * cos1))
+        waves = []
+        for p, (far_r, far_i) in zip(members(g), both_sides_of(exits, high, low, 0)):
+            misfit = far_r * far_r + far_i * far_i - meas_ref[p]
+            scale = (4.0 * LOSS_WEIGHT) * misfit
+            waves.append((scale * far_r, scale * far_i))
+        waves = both_sides_of(waves, high, low, 1)
+        for p, (g_r, g_i), (cos1, sin1), (exit_r, exit_i) in zip(members(g), waves, turns, exits):
+            back[p, 0] = g_r * cos1 + g_i * sin1
+            back[p, 1] = g_i * cos1 - g_r * sin1
+            paste(p, SIGMA * (g_i * exit_r - g_r * exit_i))
+        return carry
+
+    def backward(g, carry):
+        waves = both_sides_of([(back[p, 0], back[p, 1]) for p in members(g)], high, low, 3)
+        for p, (g_r, g_i) in zip(members(g), waves):
+            paste(p, SIGMA * (g_i * first[p, 0] - g_r * first[p, 1]))
         return carry
 
     def rows(who):
@@ -519,10 +574,19 @@
     def to_peer(s, side, j):
         kind = 2 * chips + side * (chips - 1) + j - 1
         device = {"owner": (owner + 2 * j) % owners}
-        return r_copy(s, kind, total.at[s, side, j - 1], far.at[s, side, j - 1], device)
+        at = (s, side, j - 1)
+        more = kind + 2 * chips - 1
+        return Several(
+            r_copy(s, kind, total.at[at], far.at[at], device),
+            r_copy(s, more, total_scale.at[at], far_scale.at[at], device),
+        )
 
     def to_right(s):
-        return r_copy(s, 4 * chips - 2, edge.at[s], edge_in.at[s], {"tile": tile + 1})
+        device = {"tile": tile + 1}
+        return Several(
+            r_copy(s, 4 * chips - 2, edge.at[s], edge_in.at[s], device),
+            r_copy(s, 6 * chips - 3, edge_scale.at[s], edge_in_scale.at[s], device),
+        )
 
     def block_sum(who, side):
         starts = [place_ref[p, 4 + who] for p in range(probes)]
@@ -549,7 +613,9 @@
             for j in peers:
                 to_partner(s, side, j).wait_recv()
                 mine = grad[s, rows((owner + 2 * j) % owners), cols(side)]
-                total[s, side, j - 1] = mine + near[s, side, j]
+                code, scale = encode(mine + near[s, side, j])
+                total[s, side, j - 1] = code
+                total_scale[s, side, j - 1] = scale
                 to_peer(s, side, j).start()
 
     def collect(s, side):
@@ -557,27 +623,35 @@
         value = grad[s, rows(owner), cols(side)] + near[s, side, 0]
         for j in peers:
             to_peer(s, side, j).wait_recv()
-            value = value + far[s, side, j - 1]
+            value = value + decode(far[s, side, j - 1], far_scale[s, side, j - 1])
         if side == 1:
-            edge[s] = value
+            edge[s], edge_scale[s] = encode(value)
             pl.when(has_right)(lambda: to_right(s).start())
         else:
             out_ref[s] = value
 
     def add_edge(s):
         to_right(s).wait_recv()
-        out_ref[s] += edge_in[s]
-
-    lax.fori_loop(0, probes, forward, 0)
+        out_ref[s] += decode(edge_in[s], edge_in_scale[s])
+
+    groups_all = probes // GROUP
+    lax.fori_loop(0, 1, enter, 0)
+    pass_on(1, 0)
+    pl.when(has_right)(lambda: pass_on(1, 1))
+    lax.fori_loop(1, groups_all, enter, 0)
+    landed(1, 0)
+    pl.when(has_right)(lambda: landed(1, 1))
+    lax.fori_loop(0, groups_all, forward, 0)
     give(1)
     lax.fori_loop(0, 1, backward, 0)
     across(1)
-    lax.fori_loop(1, probes, backward, 0)
+    lax.fori_loop(1, groups_all, backward, 0)
+    collect(1, 1)
     give(0)
     across(0)
-    for side in (1, 0):
-        for s in (1, 0):
-            collect(s, side)
+    collect(1, 0)
+    collect(0, 1)
+    collect(0, 0)
     for s in (1, 0):
         pl.when(has_left)(lambda s=s: add_edge(s))
 
@@ -631,15 +705,19 @@
             pltpu.VMEM((probes, (2 * size + width) // 8 + 1, 8, 2 * width), f32),
             pltpu.VMEM((layers, owners * size, 2 * width), f32),
             pltpu.VMEM((layers, 2, chips) + block, f32),
-            pltpu.VMEM((layers, 2, peers) + block, f32),
-            pltpu.VMEM((layers, 2, peers) + block, f32),
-            pltpu.VMEM((layers,) + block, f32),
-            pltpu.VMEM((layers,) + block, f32),
+            pltpu.VMEM((layers, 2, peers) + block, jnp.int16),
+            pltpu.VMEM((layers, 2, peers) + block, jnp.int16),
+            pltpu.VMEM((layers,) + block, jnp.int16),
+            pltpu.VMEM((layers,) + block, jnp.int16),
+            pltpu.VMEM((layers, 2, peers, 8, width), f32),
+            pltpu.VMEM((layers, 2, peers, 8, width), f32),
+            pltpu.VMEM((layers, 8, width), f32),
+            pltpu.VMEM((layers, 8, width), f32),
             pltpu.SemaphoreType.DMA((3,)),
             pltpu.SemaphoreType.DMA((layers, 3 + 4 * (chips - 1))),
             pltpu.SemaphoreType.DMA((layers, 3 + 4 * (chips - 1))),
-            pltpu.SemaphoreType.DMA((layers, 4 * chips - 1)),
-            pltpu.SemaphoreType.DMA((layers, 4 * chips - 1)),
+            pltpu.SemaphoreType.DMA((layers, 6 * chips - 2)),
+            pltpu.SemaphoreType.DMA((layers, 6 * chips - 2)),
         ],
         compiler_params=pltpu.CompilerParams(
             collective_id=2, has_side_effects=True, vmem_limit_bytes=56 * 2**20
@@ -655,7 +733,7 @@
     tile_rows = rows_part.shape[1] * lax.axis_size("owner")
     tile_cols = rows_part.shape[2]
     below = lax.axis_size("tile") > TX
-    if not below and layers == 2:
+    if not below and layers == 2 and measured.shape[0] % GROUP == 0:
         return fused(rows_part, positions, illumination, measured)[:, None]
     extended = gather_grid(rows_part)
     if below:

time: 78.7 us -> 58.7 us (0.75)
  Pallas kernels: 73.8 us -> 54.1 us
    pallas_call x1, Pallas kernels: 73.8 us -> 54.1 us  [fused(): pl.pallas_call(functools.partial(fused_kernel, owners), out_shape=jax.Sha...]
where the time goes in v3:
time: 58.7 us; the launch traced here: 57.8 us
  Pallas kernels  54.1 us (92%)
  local copies, waits for them, and re-layouts  3.48 us (6%)
    pallas_call x1, Pallas kernels, fused(): pl.pallas_call(functools.partial(fused_kernel, owners), out_shape=jax.Sha...  54.1 us
    unnamed x3, local copies, waits for them, and re-layouts  2.06 us

profile of v3, /device:TPU:0, one launch (start us, length us, event | category | flops | bytes accessed | tf_op | source)
XLA Modules:
  0.0 57.8 jit_solution(18211832039709700908)
XLA Ops:
  0.0 0.8 %fusion.10 = (s32[4,1]{0,1:T(1,128)S(1)}, s32[4,1]{0,1:T(1,128)S(1)}) fusion(s32[4,2]{0,1:T(2,128)} %param.7), kind=kLoop, calls=%fused_computation.34 | loop fusion | bytes 64 | tf_op jit(solution)/shard_map/slice | solution.py:679
  0.8 0.1 copy.14
  0.9 0.1 copy.13
  0.9 0.1 fusion.5
  1.1 0.1 add_select_fusion
  1.2 0.7 %concatenate.3.place_ref = s32[4,8]{1,0:T(4,128)} concatenate(s32[4,1]{1,0:T(4,128)S(1)} %get-tuple-element.8, s32[4,1]{1,0:T(4,128)S(1)} %get-tuple-element.6, s32[4,1]{1,0:T(4,128)S(1)} %get-tuple-element.11, s32[4,1]{1,0:T(4,128)S(1)} %get-tuple-element.7, s32[4,4]{1,0:T(4,128)S(1)} %add_select_fusion), dimensions={1} | concatenate | bytes 256 | tf_op jit(solution)/shard_map/concatenate | solution.py:684
  1.8 54.1 %shard_map.64 = f32[2,256,256]{2,1,0:T(8,128)} custom-call(s32[4,8]{1,0:T(4,128)} %concatenate.3.place_ref, bf16[2,16,16,256]{3,2,1,0:T(8,128)(2,1)} %bitcast.5, f32[2,256,256]{2,1,0:T(8,128)} %illum_ref.1, f32[4,256,256]{2,1,0:T(8,128)} %meas_hbm.1, bf16[4,512,512]{2,1,0:T(8,128)(2,1)} %constant.93.clone.high_hbm, bf16[4,512,512]{2,1,0:T(8,128)(2,1)} %constant.94.clone.low_hbm), custom_call_target="tpu_custom_call" | custom-call | flops 12884901888 | bytes 8388608 | tf_op jit(solution)/shard_map/pallas_call | solution.py:692
  56.0 1.9 %copy.16 = f32[2,1,256,256]{3,2,1,0:T(8,128)} copy(f32[2,1,256,256]{3,2,1,0:T(8,128)} %bitcast.4) | data formatting | bytes 1048576
  (1 shorter events, 0.0 us)

commit v4 on v3

--- a/solution.py
+++ b/solution.py
@@ -65,16 +65,27 @@
     return tall[:width], tall[width:]
 
 
-def both_sides_of(waves, high, low, which):
+def triple_tables(width):
+    high, low = block_tables(width)
+    right = np.concatenate([high, high, low], axis=1)
+    left = np.concatenate([high, low, high], axis=2)
+    return jnp.asarray(right), jnp.asarray(left)
+
+
+def both_sides_of(waves, right, left, which):
     width = waves[0][0].shape[0]
+
+    def dot(x, y):
+        return jnp.dot(x, y, preferred_element_type=jnp.float32)
+
     wide = jnp.concatenate([jnp.concatenate(wave, axis=1) for wave in waves], axis=0)
-    wide = dot3(halves(wide), (high[which], low[which]))
+    a, b = halves(wide)
+    wide = dot(jnp.concatenate([a, b, a], axis=1), right[which])
     spans = [slice(k * width, (k + 1) * width) for k in range(len(waves))]
     real = jnp.concatenate([wide[span, :width] for span in spans], axis=1)
     imag = jnp.concatenate([wide[span, width:] for span in spans], axis=1)
-    tall = jnp.concatenate([real, imag], axis=0)
-    other = which ^ 1
-    tall = dot3((high[other], low[other]), halves(tall))
+    a, b = halves(jnp.concatenate([real, imag], axis=0))
+    tall = dot(left[which ^ 1], jnp.concatenate([a, a, b], axis=0))
     return [(tall[:width, span], tall[width:, span]) for span in spans]
 
 
@@ -392,8 +403,8 @@
 
 
 def fused_kernel(
-    owners, place_ref, part_ref, illum_ref, meas_hbm, high_hbm, low_hbm, out_ref,
-    ext0, ext1, meas_ref, high, low, first, back, pads, grad, near, total, far, edge, edge_in,
+    owners, place_ref, part_ref, illum_ref, meas_hbm, right_hbm, left_hbm, out_ref,
+    ext0, ext1, meas_ref, right, left, first, back, pads, grad, near, total, far, edge, edge_in,
     total_scale, far_scale, edge_scale, edge_in_scale, loads, g_send, g_recv, sends, recvs,
 ):
     tile, owner, partner, has_left, has_right = places()
@@ -410,7 +421,7 @@
 
     fetches = [
         pltpu.make_async_copy(src, dst, loads.at[i])
-        for i, (src, dst) in enumerate(((high_hbm, high), (low_hbm, low), (meas_hbm, meas_ref)))
+        for i, (src, dst) in enumerate(((right_hbm, right), (left_hbm, left), (meas_hbm, meas_ref)))
     ]
     for fetch in fetches:
         fetch.start()
@@ -469,8 +480,7 @@
         g_left(s).wait_recv()
         spread(s, 1)
 
-    for s in range(layers):
-        pl.when(has_left)(lambda s=s: g_left(s).start())
+    pl.when(has_left)(lambda: g_left(0).start())
     spread(0, 0)
     blank = jnp.zeros((probes, size // 8, 8, cols_all), jnp.float32)
     pads[:, : size // 8] = blank
@@ -483,12 +493,13 @@
             ext[s][:, :, width:] = jnp.zeros((rows_all // ALIGN, ALIGN, width), part_ref.dtype)
 
     pl.when(has_right)(lambda: right_spread(0))
+    pl.when(has_left)(lambda: g_left(1).start())
     spread(1, 0)
     pass_on(0, 0)
     pl.when(has_right)(lambda: pass_on(0, 1))
-    pl.when(has_right)(lambda: right_spread(1))
     landed(0, 0)
     pl.when(has_right)(lambda: landed(0, 1))
+    pl.when(has_right)(lambda: right_spread(1))
     for fetch in fetches:
         fetch.wait()
 
@@ -524,7 +535,7 @@
             first[p, 0] = illum_ref[0] * cos0 - illum_ref[1] * sin0
             first[p, 1] = illum_ref[0] * sin0 + illum_ref[1] * cos0
             waves.append((first[p, 0], first[p, 1]))
-        waves = both_sides_of(waves, high, low, 2)
+        waves = both_sides_of(waves, right, left, 2)
         for p, (real, imag) in zip(members(g), waves):
             back[p, 0] = real
             back[p, 1] = imag
@@ -538,11 +549,11 @@
             turns.append((cos1, sin1))
             exits.append((mid_r * cos1 - mid_i * sin1, mid_r * sin1 + mid_i * cos1))
         waves = []
-        for p, (far_r, far_i) in zip(members(g), both_sides_of(exits, high, low, 0)):
+        for p, (far_r, far_i) in zip(members(g), both_sides_of(exits, right, left, 0)):
             misfit = far_r * far_r + far_i * far_i - meas_ref[p]
             scale = (4.0 * LOSS_WEIGHT) * misfit
             waves.append((scale * far_r, scale * far_i))
-        waves = both_sides_of(waves, high, low, 1)
+        waves = both_sides_of(waves, right, left, 1)
         for p, (g_r, g_i), (cos1, sin1), (exit_r, exit_i) in zip(members(g), waves, turns, exits):
             back[p, 0] = g_r * cos1 + g_i * sin1
             back[p, 1] = g_i * cos1 - g_r * sin1
@@ -550,7 +561,7 @@
         return carry
 
     def backward(g, carry):
-        waves = both_sides_of([(back[p, 0], back[p, 1]) for p in members(g)], high, low, 3)
+        waves = both_sides_of([(back[p, 0], back[p, 1]) for p in members(g)], right, left, 3)
         for p, (g_r, g_i) in zip(members(g), waves):
             paste(p, SIGMA * (g_i * first[p, 0] - g_r * first[p, 1]))
         return carry
@@ -673,7 +684,7 @@
     probes = measured.shape[0]
     chips = owners // 2
     peers = max(chips - 1, 1)
-    high, low = block_tables(width)
+    right, left = triple_tables(width)
     tile = lax.axis_index("tile")
     row = positions[:, 0] - tile // TX * (owners * size)
     col = positions[:, 1] - tile % TX * width
@@ -698,8 +709,8 @@
             pltpu.VMEM((owners * size // ALIGN, ALIGN, 2 * width), rows_part.dtype),
             pltpu.VMEM((owners * size // ALIGN, ALIGN, 2 * width), rows_part.dtype),
             pltpu.VMEM(measured.shape, f32),
-            pltpu.VMEM(high.shape, jnp.bfloat16),
-            pltpu.VMEM(low.shape, jnp.bfloat16),
+            pltpu.VMEM(right.shape, jnp.bfloat16),
+            pltpu.VMEM(left.shape, jnp.bfloat16),
             pltpu.VMEM((probes, 2, width, width), f32),
             pltpu.VMEM((probes, 2, width, width), f32),
             pltpu.VMEM((probes, (2 * size + width) // 8 + 1, 8, 2 * width), f32),
@@ -723,7 +734,7 @@
             collective_id=2, has_side_effects=True, vmem_limit_bytes=56 * 2**20
         ),
         cost_estimate=pl.CostEstimate(flops=flops, bytes_accessed=8 * 2**20, transcendentals=0),
-    )(place, grouped, illumination, measured, jnp.asarray(high), jnp.asarray(low))
+    )(place, grouped, illumination, measured, right, left)
 
 
 def body(potential, positions, illumination, measured):

time: 58.7 us -> 58.3 us (level)
  no operation moved by 1% of the time
where the time goes in v4:
time: 58.3 us; the launch traced here: 57.3 us
  Pallas kernels  53.6 us (92%)
  local copies, waits for them, and re-layouts  3.48 us (6%)
    pallas_call x1, Pallas kernels, fused(): pl.pallas_call(functools.partial(fused_kernel, owners), out_shape=jax.Sha...  53.6 us
    unnamed x3, local copies, waits for them, and re-layouts  2.06 us

profile of v4, /device:TPU:0, one launch (start us, length us, event | category | flops | bytes accessed | tf_op | source)
XLA Modules:
  0.0 57.3 jit_solution(13390350041891961941)
XLA Ops:
  0.0 0.8 %fusion.10 = (s32[4,1]{0,1:T(1,128)S(1)}, s32[4,1]{0,1:T(1,128)S(1)}) fusion(s32[4,2]{0,1:T(2,128)} %param.7), kind=kLoop, calls=%fused_computation.34 | loop fusion | bytes 64 | tf_op jit(solution)/shard_map/slice | solution.py:690
  0.8 0.1 copy.14
  0.9 0.1 copy.13
  0.9 0.1 fusion.5
  1.1 0.1 add_select_fusion
  1.2 0.7 %concatenate.3.place_ref = s32[4,8]{1,0:T(4,128)} concatenate(s32[4,1]{1,0:T(4,128)S(1)} %get-tuple-element.8, s32[4,1]{1,0:T(4,128)S(1)} %get-tuple-element.6, s32[4,1]{1,0:T(4,128)S(1)} %get-tuple-element.11, s32[4,1]{1,0:T(4,128)S(1)} %get-tuple-element.7, s32[4,4]{1,0:T(4,128)S(1)} %add_select_fusion), dimensions={1} | concatenate | bytes 256 | tf_op jit(solution)/shard_map/concatenate | solution.py:695
  1.8 53.6 %shard_map.64 = f32[2,256,256]{2,1,0:T(8,128)} custom-call(s32[4,8]{1,0:T(4,128)} %concatenate.3.place_ref, bf16[2,16,16,256]{3,2,1,0:T(8,128)(2,1)} %bitcast.5, f32[2,256,256]{2,1,0:T(8,128)} %illum_ref.1, f32[4,256,256]{2,1,0:T(8,128)} %meas_hbm.1, bf16[4,1536,512]{2,1,0:T(8,128)(2,1)} %constant.93.clone.right_hbm, ...), custom_call_target="tpu_custom_call" | custom-call | flops 12884901888 | bytes 8388608 | tf_op jit(solution)/shard_map/pallas_call | solution.py:703
  55.5 1.9 %copy.16 = f32[2,1,256,256]{3,2,1,0:T(8,128)} copy(f32[2,1,256,256]{3,2,1,0:T(8,128)} %bitcast.4) | data formatting | bytes 1048576
  (1 shorter events, 0.0 us)

commit v5 on v4

--- a/solution.py
+++ b/solution.py
@@ -566,11 +566,14 @@
             paste(p, SIGMA * (g_i * first[p, 0] - g_r * first[p, 1]))
         return carry
 
+    part = width // 2
+    right_sides, left_sides = (3, 2), (1, 0)
+
     def rows(who):
         return pl.ds(pl.multiple_of(who * size, size), size)
 
     def cols(side):
-        return pl.ds(side * width, width)
+        return pl.ds(side * part, part)
 
     def r_copy(s, kind, src, dst, device):
         return pltpu.make_async_remote_copy(
@@ -583,20 +586,21 @@
         return r_copy(s, side * chips + j, src, near.at[s, side, j], {"owner": partner})
 
     def to_peer(s, side, j):
-        kind = 2 * chips + side * (chips - 1) + j - 1
+        kind = 4 * chips + side * (chips - 1) + j - 1
         device = {"owner": (owner + 2 * j) % owners}
         at = (s, side, j - 1)
-        more = kind + 2 * chips - 1
+        more = kind + 4 * (chips - 1)
         return Several(
             r_copy(s, kind, total.at[at], far.at[at], device),
             r_copy(s, more, total_scale.at[at], far_scale.at[at], device),
         )
 
-    def to_right(s):
+    def to_right(s, side):
+        kind = 12 * chips - 8 + 2 * (side - 2)
         device = {"tile": tile + 1}
         return Several(
-            r_copy(s, 4 * chips - 2, edge.at[s], edge_in.at[s], device),
-            r_copy(s, 6 * chips - 3, edge_scale.at[s], edge_in_scale.at[s], device),
+            r_copy(s, kind, edge.at[s, side - 2], edge_in.at[s, side - 2], device),
+            r_copy(s, kind + 1, edge_scale.at[s, side - 2], edge_in_scale.at[s, side - 2], device),
         )
 
     def block_sum(who, side):
@@ -609,18 +613,18 @@
         return value
 
     def give(s):
-        for side in (1, 0):
+        for side in right_sides + left_sides:
             for j in peers + [0]:
                 who = (partner + 2 * j) % owners
                 grad[s, rows(who), cols(side)] = block_sum(who, side)
                 to_partner(s, side, j).start()
-        for side in (1, 0):
+        for side in right_sides + left_sides:
             for j in peers + [0]:
                 who = (owner + 2 * j) % owners
                 grad[s, rows(who), cols(side)] = block_sum(who, side)
 
     def across(s):
-        for side in (1, 0):
+        for side in right_sides + left_sides:
             for j in peers:
                 to_partner(s, side, j).wait_recv()
                 mine = grad[s, rows((owner + 2 * j) % owners), cols(side)]
@@ -635,15 +639,17 @@
         for j in peers:
             to_peer(s, side, j).wait_recv()
             value = value + decode(far[s, side, j - 1], far_scale[s, side, j - 1])
-        if side == 1:
-            edge[s], edge_scale[s] = encode(value)
-            pl.when(has_right)(lambda: to_right(s).start())
+        if side in right_sides:
+            edge[s, side - 2], edge_scale[s, side - 2] = encode(value)
+            pl.when(has_right)(lambda: to_right(s, side).start())
         else:
-            out_ref[s] = value
+            out_ref[s, :, cols(side)] = value
 
     def add_edge(s):
-        to_right(s).wait_recv()
-        out_ref[s] += decode(edge_in[s], edge_in_scale[s])
+        for side in right_sides:
+            to_right(s, side).wait_recv()
+            add = decode(edge_in[s, side - 2], edge_in_scale[s, side - 2])
+            out_ref[s, :, cols(side - 2)] += add
 
     groups_all = probes // GROUP
     lax.fori_loop(0, 1, enter, 0)
@@ -657,12 +663,14 @@
     lax.fori_loop(0, 1, backward, 0)
     across(1)
     lax.fori_loop(1, groups_all, backward, 0)
-    collect(1, 1)
+    for side in right_sides:
+        collect(1, side)
     give(0)
     across(0)
-    collect(1, 0)
-    collect(0, 1)
-    collect(0, 0)
+    for side in left_sides:
+        collect(1, side)
+    for side in right_sides + left_sides:
+        collect(0, side)
     for s in (1, 0):
         pl.when(has_left)(lambda s=s: add_edge(s))
 
@@ -670,12 +678,13 @@
         sent(s, 0)
         pl.when(has_right)(lambda s=s: sent(s, 1))
         pl.when(has_left)(lambda s=s: g_left(s).wait_send())
-        for side in (0, 1):
+        for side in right_sides + left_sides:
             for j in peers + [0]:
                 to_partner(s, side, j).wait_send()
             for j in peers:
                 to_peer(s, side, j).wait_send()
-        pl.when(has_right)(lambda s=s: to_right(s).wait_send())
+        for side in right_sides:
+            pl.when(has_right)(lambda s=s, side=side: to_right(s, side).wait_send())
 
 
 def fused(rows_part, positions, illumination, measured):
@@ -698,6 +707,7 @@
     vmem = pl.BlockSpec(memory_space=pltpu.VMEM)
     anywhere = pl.BlockSpec(memory_space=pl.ANY)
     block = (size, width)
+    chunk = (size, width // 2)
     f32 = jnp.float32
     flops = probes * 4 * 2 * 3 * 2 * (2 * width) ** 2 * width
     return pl.pallas_call(
@@ -715,20 +725,20 @@
             pltpu.VMEM((probes, 2, width, width), f32),
             pltpu.VMEM((probes, (2 * size + width) // 8 + 1, 8, 2 * width), f32),
             pltpu.VMEM((layers, owners * size, 2 * width), f32),
-            pltpu.VMEM((layers, 2, chips) + block, f32),
-            pltpu.VMEM((layers, 2, peers) + block, jnp.int16),
-            pltpu.VMEM((layers, 2, peers) + block, jnp.int16),
-            pltpu.VMEM((layers,) + block, jnp.int16),
-            pltpu.VMEM((layers,) + block, jnp.int16),
-            pltpu.VMEM((layers, 2, peers, 8, width), f32),
-            pltpu.VMEM((layers, 2, peers, 8, width), f32),
-            pltpu.VMEM((layers, 8, width), f32),
-            pltpu.VMEM((layers, 8, width), f32),
+            pltpu.VMEM((layers, 4, chips) + chunk, f32),
+            pltpu.VMEM((layers, 4, peers) + chunk, jnp.int16),
+            pltpu.VMEM((layers, 4, peers) + chunk, jnp.int16),
+            pltpu.VMEM((layers, 2) + chunk, jnp.int16),
+            pltpu.VMEM((layers, 2) + chunk, jnp.int16),
+            pltpu.VMEM((layers, 4, peers, 8, width // 2), f32),
+            pltpu.VMEM((layers, 4, peers, 8, width // 2), f32),
+            pltpu.VMEM((layers, 2, 8, width // 2), f32),
+            pltpu.VMEM((layers, 2, 8, width // 2), f32),
             pltpu.SemaphoreType.DMA((3,)),
             pltpu.SemaphoreType.DMA((layers, 3 + 4 * (chips - 1))),
             pltpu.SemaphoreType.DMA((layers, 3 + 4 * (chips - 1))),
-            pltpu.SemaphoreType.DMA((layers, 6 * chips - 2)),
-            pltpu.SemaphoreType.DMA((layers, 6 * chips - 2)),
+            pltpu.SemaphoreType.DMA((layers, 12 * chips - 4)),
+            pltpu.SemaphoreType.DMA((layers, 12 * chips - 4)),
         ],
         compiler_params=pltpu.CompilerParams(
             collective_id=2, has_side_effects=True, vmem_limit_bytes=56 * 2**20

time: 58.3 us -> 57.7 us (0.990); the launches traced: 57.3 us -> 57.5 us
  no operation moved by 1% of the time
where the time goes in v5:
time: 57.7 us; the launch traced here: 57.5 us
  Pallas kernels  53.7 us (93%)
  local copies, waits for them, and re-layouts  3.48 us (6%)
    pallas_call x1, Pallas kernels, fused(): pl.pallas_call(functools.partial(fused_kernel, owners), out_shape=jax.Sha...  53.7 us
    unnamed x3, local copies, waits for them, and re-layouts  2.06 us

profile of v5, /device:TPU:0, one launch (start us, length us, event | category | flops | bytes accessed | tf_op | source)
XLA Modules:
  0.0 57.5 jit_solution(9220935471403054460)
XLA Ops:
  0.0 0.8 %fusion.10 = (s32[4,1]{0,1:T(1,128)S(1)}, s32[4,1]{0,1:T(1,128)S(1)}) fusion(s32[4,2]{0,1:T(2,128)} %param.7), kind=kLoop, calls=%fused_computation.34 | loop fusion | bytes 64 | tf_op jit(solution)/shard_map/slice | solution.py:699
  0.8 0.1 copy.14
  0.9 0.1 copy.13
  0.9 0.1 fusion.5
  1.1 0.1 add_select_fusion
  1.2 0.7 %concatenate.3.place_ref = s32[4,8]{1,0:T(4,128)} concatenate(s32[4,1]{1,0:T(4,128)S(1)} %get-tuple-element.8, s32[4,1]{1,0:T(4,128)S(1)} %get-tuple-element.6, s32[4,1]{1,0:T(4,128)S(1)} %get-tuple-element.11, s32[4,1]{1,0:T(4,128)S(1)} %get-tuple-element.7, s32[4,4]{1,0:T(4,128)S(1)} %add_select_fusion), dimensions={1} | concatenate | bytes 256 | tf_op jit(solution)/shard_map/concatenate | solution.py:704
  1.8 53.7 %shard_map.64 = f32[2,256,256]{2,1,0:T(8,128)} custom-call(s32[4,8]{1,0:T(4,128)} %concatenate.3.place_ref, bf16[2,16,16,256]{3,2,1,0:T(8,128)(2,1)} %bitcast.5, f32[2,256,256]{2,1,0:T(8,128)} %illum_ref.1, f32[4,256,256]{2,1,0:T(8,128)} %meas_hbm.1, bf16[4,1536,512]{2,1,0:T(8,128)(2,1)} %constant.93.clone.right_hbm, ...), custom_call_target="tpu_custom_call" | custom-call | flops 12884901888 | bytes 8388608 | tf_op jit(solution)/shard_map/pallas_call | solution.py:713
  55.6 1.9 %copy.16 = f32[2,1,256,256]{3,2,1,0:T(8,128)} copy(f32[2,1,256,256]{3,2,1,0:T(8,128)} %bitcast.4) | data formatting | bytes 1048576
  (1 shorter events, 0.0 us)
